TPU v7x, 32 devices: a whole 2x2x4 slice. The times are simulated.
32 devices in a mesh: rep: 8 (over y, x, core), head: 4 (over z).
Axes of the slice: x: 2, y: 2, z: 4, core: 2. Of those that a mesh axis runs over, the one named last changes fastest.
Arguments:
- ssd_x: bfloat16 [512, 4096], P('rep', 'head'), may hold values from -6 to 6
- gate_z: bfloat16 [512, 4096], P('rep', 'head'), may hold values from -6 to 6
- group_b: bfloat16 [512, 512], P('rep', 'head'), may hold values from -6 to 6
- group_c: bfloat16 [512, 512], P('rep', 'head'), may hold values from -0.5 to 0.5
- step_dt: bfloat16 [512, 64], P('rep', 'head'), may hold values from 0.5 to 2
- queries: bfloat16 [512, 4096], P('rep', 'head'), may hold values from -8 to 8
- tail_kv: bfloat16 [512, 1024], P('rep', 'head'), may hold values from -6 to 6
- ckpt_state: bfloat16 [32, 64, 64, 128], P('rep', 'head'), may hold values from -6 to 6
- kv_pool: bfloat16 [512, 16, 1024], P('rep', None, 'head'), may hold values from -8 to 8
- w_out: bfloat16 [4096, 4096], P('head', 'rep'), may hold values from -0.125 to 0.125
- decay_rate: float32 [64], P('head'), may hold values from 0.002 to 2
- skip_d: float32 [64], P('head'), may hold values from 0.5 to 1.5
- norm_gain: float32 [4096], P('head'), may hold values from 0.5 to 1.5
- owner: int32 [32], replicated, may hold values from 0 to 7, as said below
- slot: int32 [32], replicated, may hold values from 0 to 3, as said below
- page_table: int32 [32, 16], replicated, may hold values from 0 to 63, as said below
- hit_len: int32 [32], replicated, may hold values from 2 to 256, as said below
- tail_len: int32 [32], replicated, may hold values from 1 to 16, as said below
Outputs:
- ssd_out: bfloat16 [512, 4096], P('rep', 'head')
- attn_proj: bfloat16 [512, 4096], P('rep', 'head')
- final_state: bfloat16 [32, 64, 64, 128], P('rep', 'head')
Inputs may be any that keep to these rules, and one draw needn't show every extreme that they name: Every replica owns exactly 4 requests, and no two requests of one replica share an owner. `slot`: the requests of one owner have distinct slots. `page_table`: each of an owner's 64 pages belongs to exactly one of its requests. `hit_len`: some request has exactly 256. `tail_len`: some request has exactly 16.
All inputs are finite; a program needn't handle non-finite values.
Results may differ from a plain program's by a relative error of at most 0.0057.
Values may be sent and summed in bfloat16 or wider, within the bound.
A program may use at most 192 MiB of HBM per device.

v0:
```python
import math

import jax
import jax.numpy as jnp
from jax import lax
from jax.sharding import PartitionSpec as P

TAIL = 16
STATE = 128
QH_DEV = 8
DH = 128


highest = lax.Precision.HIGHEST


def scan_heads(signal, b_rows, c_rows, step_sizes, state_start, rates, skipping, alive):
    length = signal.shape[1]
    head_count = signal.shape[2]
    fanout = head_count // b_rows.shape[2]
    log_decay = -rates[None, None, :] * step_sizes * alive[:, :, None]
    running = jnp.cumsum(log_decay, axis=1)
    position = jnp.arange(length, dtype=jnp.int32)
    causal = (position[:, None] >= position[None, :])[None, :, :, None]
    spans = running[:, :, None, :] - running[:, None, :, :]
    decays = jnp.where(causal, jnp.exp(jnp.where(causal, spans, 0.0)), 0.0)
    intersection = jnp.einsum("ktgn,kugn->ktug", c_rows, b_rows, precision=highest)
    intersection_head = jnp.repeat(intersection, fanout, axis=3)
    weighted_dt = step_sizes * alive[:, :, None]
    mixing = decays * intersection_head * weighted_dt[:, None, :, :]
    within = jnp.einsum("ktue,kuep->ktep", mixing, signal, precision=highest)
    c_heads = jnp.repeat(c_rows, fanout, axis=2)
    b_heads = jnp.repeat(b_rows, fanout, axis=2)
    from_state = jnp.exp(running)[..., None] * jnp.einsum(
        "kten,kepn->ktep", c_heads, state_start, precision=highest
    )
    mixer = (within + from_state + skipping[None, None, :, None] * signal) * alive[:, :, None, None]
    last_cum = running[:, -1, :]
    weights_in = jnp.exp(last_cum[:, None, :] - running) * weighted_dt
    closing = jnp.exp(last_cum)[:, :, None, None] * state_start + jnp.einsum(
        "kue,kuen,kuep->kepn", weights_in, b_heads, signal, precision=highest
    )
    return (mixer, closing)


def attend(query_rows, cached, tail_rows, hit_sizes, tail_sizes, alive):
    batch = query_rows.shape[0]
    query_len = query_rows.shape[1]
    cache_len = cached.shape[1]
    scaling = 1.0 / math.sqrt(query_rows.shape[-1])
    cached_scores = (
        jnp.einsum(
            "ktaqd,kcad->ktaqc",
            query_rows,
            cached[:, :, :, 0, :],
            preferred_element_type=jnp.float32,
        )
        * scaling
    )
    tail_scores = (
        jnp.einsum(
            "ktaqd,kuad->ktaqu",
            query_rows,
            tail_rows[:, :, :, 0, :],
            preferred_element_type=jnp.float32,
        )
        * scaling
    )
    positions = jnp.arange(cache_len, dtype=jnp.int32)
    position = jnp.arange(query_len, dtype=jnp.int32)
    seen_cache = jnp.broadcast_to(
        (positions[None, :] < hit_sizes[:, None])[:, None, :], (batch, query_len, cache_len)
    )
    seen_tail = (position[None, None, :] <= position[None, :, None]) & (
        position[None, None, :] < tail_sizes[:, None, None]
    )
    visible = jnp.concatenate([seen_cache, seen_tail], axis=2)[:, :, None, None, :]
    scores = jnp.where(visible, jnp.concatenate([cached_scores, tail_scores], axis=4), -1e30)
    row_max = jnp.max(scores, axis=4, keepdims=True)
    exponent = jnp.where(visible, jnp.exp(scores - row_max), 0.0)
    weights = (exponent / jnp.sum(exponent, axis=4, keepdims=True)).astype(jnp.bfloat16)
    result = jnp.einsum(
        "ktaqc,kcad->ktaqd",
        weights[..., :cache_len],
        cached[:, :, :, 1, :],
        preferred_element_type=jnp.float32,
    )
    result = result + jnp.einsum(
        "ktaqu,kuad->ktaqd",
        weights[..., cache_len:],
        tail_rows[:, :, :, 1, :],
        preferred_element_type=jnp.float32,
    )
    return (result * alive[:, :, None, None, None]).astype(jnp.bfloat16)


def spread(selector, values):
    flat = values.reshape(values.shape[0], -1)
    mixed = jnp.dot(selector, flat, preferred_element_type=jnp.float32)
    return mixed.astype(values.dtype).reshape((selector.shape[0],) + values.shape[1:])


def local(
    ssd_x,
    gate_z,
    group_b,
    group_c,
    step_dt,
    queries,
    tail_kv,
    ckpt_state,
    kv_pool,
    w_out,
    decay_rate,
    skip_d,
    norm_gain,
    owner,
    slot,
    page_table,
    hit_len,
    tail_len,
):
    replicas = lax.axis_size("rep")
    myself = lax.axis_index("rep")
    slot_count = ckpt_state.shape[0]
    head_count = ckpt_state.shape[1]
    head_size = ckpt_state.shape[2]
    group_width = head_count * head_size
    kv_columns = tail_kv.shape[1]
    kv_heads = kv_columns // (2 * DH)
    homes = jnp.arange(replicas, dtype=jnp.int32)
    slot_range = jnp.arange(slot_count, dtype=jnp.int32)
    owner_grid = owner.reshape(replicas, slot_count)
    slot_grid = slot.reshape(replicas, slot_count)
    hit_grid = hit_len.reshape(replicas, slot_count)
    tail_grid = tail_len.reshape(replicas, slot_count)
    page_grid = page_table.reshape(replicas, slot_count, -1)
    is_mine = (homes == myself)[:, None]
    my_owner = jnp.sum(jnp.where(is_mine, owner_grid, 0), axis=0)
    my_hit = jnp.sum(jnp.where(is_mine, hit_grid, 0), axis=0)
    my_tail = jnp.sum(jnp.where(is_mine, tail_grid, 0), axis=0)
    to_owner = (homes[:, None] == my_owner[None, :]).astype(jnp.bfloat16)
    holding = (
        (owner_grid == myself)[:, :, None] & (slot_grid[:, :, None] == slot_range[None, None, :])
    ).astype(jnp.int32)
    slot_home = jnp.sum(holding, axis=1).T.astype(jnp.bfloat16)
    slot_pages = jnp.sum(holding[:, :, :, None] * page_grid[:, :, None, :], axis=(0, 1))
    cache_own = kv_pool[slot_pages].reshape(slot_count, -1, kv_columns)

    def per_request(array):
        return array.reshape(slot_count, TAIL, -1)

    home_pick = slot_home.T
    fetched = (
        lax.all_to_all(
            spread(home_pick, ckpt_state), "rep", split_axis=0, concat_axis=0, tiled=True
        ),
        lax.all_to_all(
            spread(home_pick, cache_own), "rep", split_axis=0, concat_axis=0, tiled=True
        ),
    )
    owner_pick = to_owner.T
    state_start = spread(owner_pick, fetched[0])
    cached = spread(owner_pick, fetched[1])
    signal_in = per_request(ssd_x)
    batch = signal_in.shape[0]
    alive = (jnp.arange(TAIL, dtype=jnp.int32)[None, :] < my_tail[:, None]).astype(jnp.float32)
    signal = signal_in.reshape(batch, TAIL, head_count, head_size).astype(jnp.float32)
    b_rows = per_request(group_b).reshape(batch, TAIL, -1, STATE).astype(jnp.float32)
    c_rows = per_request(group_c).reshape(batch, TAIL, -1, STATE).astype(jnp.float32)
    mixer, closing = scan_heads(
        signal,
        b_rows,
        c_rows,
        per_request(step_dt).astype(jnp.float32),
        state_start.astype(jnp.float32),
        decay_rate,
        skip_d,
        alive,
    )
    gated_out = mixer * jax.nn.silu(
        per_request(gate_z).reshape(batch, TAIL, head_count, head_size).astype(jnp.float32)
    )
    energy = jnp.sum(gated_out * gated_out, axis=(2, 3))
    normed = (
        gated_out
        / jnp.sqrt(energy / group_width + 1e-05)[:, :, None, None]
        * norm_gain.reshape(head_count, head_size)
    )
    query_rows = per_request(queries).reshape(batch, TAIL, kv_heads, QH_DEV, DH)
    cached_rows = cached.reshape(batch, -1, kv_heads, 2, DH)
    tail_rows = per_request(tail_kv).reshape(batch, TAIL, kv_heads, 2, DH)
    attention = attend(query_rows, cached_rows, tail_rows, my_hit, my_tail, alive)
    ssd_rows = normed.astype(jnp.bfloat16).reshape(batch, TAIL, -1)
    attn_rows = attention.reshape(batch, TAIL, -1)
    final_rows = closing.astype(jnp.bfloat16)
    attn_flat = attn_rows.reshape(slot_count * TAIL, -1)
    terms = jnp.dot(
        attn_flat,
        lax.all_gather(w_out, "rep", axis=1, tiled=True),
        preferred_element_type=jnp.float32,
    )
    projected = lax.psum_scatter(terms, "head", scatter_dimension=1, tiled=True).astype(
        jnp.bfloat16
    )
    return (ssd_rows.reshape(slot_count * TAIL, -1), projected, final_rows)


def solution(mesh):
    return jax.shard_map(
        local,
        mesh=mesh,
        in_specs=(
            P("rep", "head"),
            P("rep", "head"),
            P("rep", "head"),
            P("rep", "head"),
            P("rep", "head"),
            P("rep", "head"),
            P("rep", "head"),
            P("rep", "head", None, None),
            P("rep", None, "head"),
            P("head", "rep"),
            P("head"),
            P("head"),
            P("head"),
            P(),
            P(),
            P(),
            P(),
            P(),
        ),
        out_specs=(P("rep", "head"), P("rep", "head"), P("rep", "head", None, None)),
        check_vma=False,
    )
```

profile of v0, /device:TPU:0, one launch (start us, length us, event | category | flops | bytes accessed | tf_op | source)
XLA Modules:
  0.0 142.8 jit_solution(868384449651795907)
XLA Ops:
  7.9 0.7 reshape.388
  8.8 0.7 eq.59
  9.6 0.8 copy.93
  12.1 1.2 copy.95
  13.3 5.2 %all-to-all-start.1 = ((bf16[8,256,256]{2,1,0:T(8,128)(2,1)}), bf16[8,256,256]{2,1,0:T(8,128)(2,1)}, u32[]{:S(2)}, u32[]{:S(2)}) async-start(bf16[8,256,256]{2,1,0:T(8,128)(2,1)} %copy.95), calls=%async_computation.1 | async-start | bytes 2097152 | tf_op jit(solution)/shard_map/all_to_all | solution.py:158
  19.4 2.3 %convolution_convert_fusion = bf16[8,131072]{1,0:T(8,128)(2,1)S(1)} fusion(bf16[1,4,1024,128]{3,2,1,0:T(8,128)(2,1)} %bitcast.129, s32[8,4]{0,1:T(4,128)S(1)} %fusion.49), kind=kOutput, calls=%fused_computation.1 | convolution fusion | flops 9437216 | bytes 3145856 | tf_op jit(solution)/shard_map/dot_general | solution.py:99
  21.9 1.9 %copy.88 = bf16[8,16,64,128]{3,2,1,0:T(8,128)(2,1)} copy(bf16[8,16,64,128]{3,0,2,1:T(8,128)(2,1)S(1)} %bitcast.122) | data formatting | bytes 4194304 | tf_op jit(solution)/shard_map/reshape | solution.py:100
  25.3 19.0 %all-to-all-done.1 = bf16[8,256,256]{2,1,0:T(8,128)(2,1)} async-done(((bf16[8,256,256]{2,1,0:T(8,128)(2,1)}), bf16[8,256,256]{2,1,0:T(8,128)(2,1)}, u32[]{:S(2)}, u32[]{:S(2)}) %all-to-all-start.1) | async-done | bytes 1048608 | tf_op jit(solution)/shard_map/all_to_all | solution.py:158
  44.3 3.6 %all-to-all-start = ((bf16[8,16,64,128]{3,2,1,0:T(8,128)(2,1)}), bf16[8,16,64,128]{3,2,1,0:T(8,128)(2,1)S(1)}, u32[]{:S(2)}, u32[]{:S(2)}) async-start(bf16[8,16,64,128]{3,2,1,0:T(8,128)(2,1)} %copy.88), calls=%async_computation | async-start | bytes 4194304 | tf_op jit(solution)/shard_map/all_to_all | solution.py:155
  48.0 1.8 %copy.115 = bf16[1,8,256,256]{3,1,2,0:T(8,128)(2,1)S(1)} copy(bf16[1,8,256,256]{3,2,1,0:T(8,128)(2,1)} %bitcast.57) | data formatting | bytes 2097152
  49.8 1.3 convolution_convert_fusion.3
  51.1 1.6 %reshape_reshape.25 = bf16[4,256,1,2,128]{4,3,1,0,2:T(2,128)(2,1)S(1)} reshape(bf16[4,65536]{1,0:T(4,128)(2,1)} %convolution_convert_fusion.3) | data formatting | bytes 1048576 | tf_op jit(solution)/shard_map/reshape;reshape | solution.py:191
  52.7 0.7 fusion.51
  54.9 44.8 %all-gather.2.cloned.1.call-done = bf16[1024,4096]{1,0:T(8,128)(2,1)} async-done(((bf16[1024,512]{1,0:T(8,128)(2,1)}), bf16[1024,4096]{1,0:T(8,128)(2,1)}) %all-gather.2.cloned.1.call-update) | async-done | bytes 8388624 | tf_op jit(solution)/shard_map/all_gather | solution.py:200
  99.7 6.0 %fusion.37 = f32[64,4096]{1,0:T(8,128)} fusion(bf16[1024,4096]{1,0:T(8,128)(2,1)} %all-gather.2.cloned.1.call-done, bf16[8,8,8,128]{3,2,1,0:T(8,128)(2,1)S(1)} %bitcast.130), kind=kOutput, calls=%fused_computation.58 | convolution fusion | flops 536870912 | bytes 9568256 | tf_op jit(solution)/shard_map/dot_general | solution.py:198
  105.8 0.7 copy.80
  108.9 1.1 reshape.406
  110.1 2.2 %convolution_bitcast_fusion.1 = f32[4,16,16,64]{3,1,2,0:T(8,128)} fusion(f32[4,16,16]{1,2,0:T(8,128)} %copy.83, f32[4,16,16]{2,1,0:T(8,128)} %copy.82, f32[4,16,16]{1,2,0:T(8,128)} %copy.80, pred[16,16]{1,0:T(8,128)(4,1)S(1)} %iota_compare_fusion.2, bf16[4,16,16,64]{3,2,1,0:T(8,128)(2,1)S(1)} %reshape_reshape.22), kind=kOutput, calls=%fused_computation.12 | convolution fusion | flops 12664832 | bytes 405760 | tf_op jit(solution)/shard_map/ktue,kuep->ktep/dot_general | solution.py:31
  112.3 6.4 %fusion.2 = bf16[1,4,1024,128]{3,1,2,0:T(4,128)(2,1)S(1)} fusion(bf16[1,8,1024,128]{3,2,1,0:T(8,128)(2,1)S(1)} %bitcast.121, s32[4]{0:T(128)S(1)} %get-tuple-element.4), kind=kOutput, calls=%fused_computation.8 | convolution fusion | flops 8912928 | bytes 3145744 | tf_op jit(solution)/shard_map/dot_general | solution.py:99
  118.9 1.8 %multiply_reduce_fusion = (f32[4,16]{1,0:T(4,128)S(1)}, f32[4,16,16,64]{3,1,2,0:T(8,128)S(1)}) fusion(f32[4,16,16,64]{3,2,1,0:T(8,128)S(1)} %reshape.406, f32[4,16]{1,0:T(4,128)S(1)} %get-tuple-element.14, bf16[4,16,16,64]{3,2,1,0:T(8,128)(2,1)S(1)} %reshape_reshape.22, f32[16]{0:T(128)S(1)} %copy-done.18, f32[4,16,16,64]{3,1,2,0:T(8,128)S(1)} %copy-done.19, ...), kind=kOutput, calls=%fused_computation.36 | convolution fusion | flops 101515200 | bytes 2003520 | tf_op jit(solution)/shard_map/kten,kepn->ktep/dot_general | solution.py:34
  121.0 0.9 reshape_reshape.23
  121.9 4.7 %add_convert_fusion = bf16[4,16,64,128]{3,2,1,0:T(8,128)(2,1)} fusion(bf16[4,16,64,128]{3,2,1,0:T(8,128)(2,1)S(1)} %bitcast.124, f32[4,16]{1,0:T(4,128)S(1)} %exp.43, f32[4,16,128]{2,1,0:T(8,128)S(1)} %convert_element_type.118, f32[4,16,16]{1,2,0:T(8,128)S(1)} %copy.103, bf16[4,16,16,64]{3,2,1,0:T(8,128)(2,1)S(1)} %reshape_reshape.22), kind=kOutput, calls=%fused_computation.7 | convolution fusion | flops 102891520 | bytes 2265344 | tf_op jit(solution)/shard_map/kue,kuen,kuep->kepn/dot_general | solution.py:40
  126.6 7.8 %reduce-scatter.2.cloned.1.call-done = f32[64,1024]{1,0:T(8,128)} async-done(((f32[64,4096]{1,0:T(8,128)}), f32[64,1024]{1,0:T(8,128)}) %reduce-scatter.2.cloned.1.call-update) | async-done | bytes 262160 | tf_op jit(solution)/shard_map/reduce_scatter | solution.py:203
  134.4 1.6 %convert_element_type.116 = bf16[64,1024]{1,0:T(8,128)(2,1)} convert(f32[64,1024]{1,0:T(8,128)} %reduce-scatter.2.cloned.1.call-done) | non-fusion elementwise | flops 65536 | bytes 393216 | tf_op jit(solution)/shard_map/convert_element_type | solution.py:203
  (100 shorter events, 9.6 us)
Async XLA Ops:
  7.2 3.4 %copy-start = (bf16[64,16,256]{2,1,0:T(8,128)(2,1)S(1)}, bf16[64,16,256]{2,1,0:T(8,128)(2,1)}, u32[]{:S(2)}) copy-start(bf16[64,16,256]{2,1,0:T(8,128)(2,1)} %param.26) | copy-start | bytes 1572868
  7.2 92.5 %all-gather.2.cloned.1.call-start = ((), (), s32[]{:S(2)}) async-start(), calls=%async_computation.3 | async-start | bytes 9437184 | tf_op jit(solution)/shard_map/all_gather | solution.py:200
  12.1 6.4 %copy-start.15 = (s32[32]{0:T(128)S(1)}, s32[32]{0:T(128)}, u32[]{:S(2)}) copy-start(s32[32]{0:T(128)} %param.35) | copy-start | bytes 388
  12.1 6.5 %copy-start.16 = (s32[32]{0:T(128)S(1)}, s32[32]{0:T(128)}, u32[]{:S(2)}) copy-start(s32[32]{0:T(128)} %param.34) | copy-start | bytes 388
  12.1 6.6 %copy-start.13 = (bf16[64,16]{0,1:T(8,128)(2,1)S(1)}, bf16[64,16]{0,1:T(8,128)(2,1)}, u32[]{:S(2)}) copy-start(bf16[64,16]{0,1:T(8,128)(2,1)} %param.22) | copy-start | bytes 6148
  12.1 6.6 %copy-start.17 = (f32[16]{0:T(128)S(1)}, f32[16]{0:T(128)}, u32[]{:S(2)}) copy-start(f32[16]{0:T(128)} %param.28) | copy-start | bytes 196
  13.3 31.0 %all-to-all-start.1 = ((bf16[8,256,256]{2,1,0:T(8,128)(2,1)}), bf16[8,256,256]{2,1,0:T(8,128)(2,1)}, u32[]{:S(2)}, u32[]{:S(2)}) async-start(bf16[8,256,256]{2,1,0:T(8,128)(2,1)} %copy.95), calls=%async_computation.1 | async-start | bytes 2097152 | tf_op jit(solution)/shard_map/all_to_all | solution.py:158
  18.5 3.2 %copy-start.7 = (bf16[64,1024]{1,0:T(8,128)(2,1)S(1)}, bf16[64,1024]{1,0:T(8,128)(2,1)}, u32[]{:S(2)}) copy-start(bf16[64,1024]{1,0:T(8,128)(2,1)} %param.23) | copy-start | bytes 393220
  18.5 3.3 %copy-start.11 = (bf16[64,256]{1,0:T(8,128)(2,1)S(1)}, bf16[64,256]{1,0:T(8,128)(2,1)}, u32[]{:S(2)}) copy-start(bf16[64,256]{1,0:T(8,128)(2,1)} %param.24) | copy-start | bytes 98308
  18.8 0.6 copy-start.4
  21.8 1.9 %copy-start.2 = (f32[4,16,16]{2,1,0:T(8,128)}, f32[4,16,16]{2,1,0:T(8,128)S(1)}, u32[]{:S(2)}) copy-start(f32[4,16,16]{2,1,0:T(8,128)S(1)} %reduce_window_sum.11) | copy-start | bytes 12292
  44.3 68.0 %all-to-all-start = ((bf16[8,16,64,128]{3,2,1,0:T(8,128)(2,1)}), bf16[8,16,64,128]{3,2,1,0:T(8,128)(2,1)S(1)}, u32[]{:S(2)}, u32[]{:S(2)}) async-start(bf16[8,16,64,128]{3,2,1,0:T(8,128)(2,1)} %copy.88), calls=%async_computation | async-start | bytes 4194304 | tf_op jit(solution)/shard_map/all_to_all | solution.py:155
  47.9 86.4 %reduce-scatter.2.cloned.1.call-start = ((), (), s32[]{:S(2)}) async-start(), calls=%async_computation.4 | async-start | bytes 1310720 | tf_op jit(solution)/shard_map/reduce_scatter | solution.py:203
  52.7 1.0 copy-start.1
  53.4 1.0 copy-start.8
  99.7 6.0 %copy-start.3 = (f32[4,16,16]{2,1,0:T(8,128)S(1)}, f32[4,16,16]{2,1,0:T(8,128)}, u32[]{:S(2)}) copy-start(f32[4,16,16]{2,1,0:T(8,128)} %copy-done.2) | copy-start | bytes 12292
  99.7 6.0 %copy-start.5 = (f32[64,16]{1,0:T(8,128)S(1)}, f32[64,16]{1,0:T(8,128)}, u32[]{:S(2)}) copy-start(f32[64,16]{1,0:T(8,128)} %copy-done.4) | copy-start | bytes 12292
  99.7 7.5 %copy-start.6 = (bf16[64,1024]{1,0:T(8,128)(2,1)S(1)}, bf16[64,1024]{1,0:T(8,128)(2,1)}, u32[]{:S(2)}) copy-start(bf16[64,1024]{1,0:T(8,128)(2,1)} %param.18) | copy-start | bytes 393220
  99.7 7.7 %copy-start.9 = (bf16[64,128]{1,0:T(8,128)(2,1)S(1)}, bf16[64,128]{1,0:T(8,128)(2,1)}, u32[]{:S(2)}) copy-start(bf16[64,128]{1,0:T(8,128)(2,1)} %param.20) | copy-start | bytes 49156
  99.7 7.7 %copy-start.10 = (bf16[64,128]{1,0:T(8,128)(2,1)S(1)}, bf16[64,128]{1,0:T(8,128)(2,1)}, u32[]{:S(2)}) copy-start(bf16[64,128]{1,0:T(8,128)(2,1)} %param.21) | copy-start | bytes 49156
  105.6 4.3 %copy-start.14 = (f32[1024]{0:T(1024)S(1)}, f32[1024]{0:T(1024)}, u32[]{:S(2)}) copy-start(f32[1024]{0:T(1024)} %param.30) | copy-start | bytes 12292
  112.3 6.6 %copy-start.12 = (f32[4,16,16]{1,2,0:T(8,128)S(1)}, f32[4,16,16]{1,2,0:T(8,128)}, u32[]{:S(2)}) copy-start(f32[4,16,16]{1,2,0:T(8,128)} %copy.85) | copy-start | bytes 12292
  112.3 6.6 %copy-start.18 = (f32[16]{0:T(128)S(1)}, f32[16]{0:T(128)}, u32[]{:S(2)}) copy-start(f32[16]{0:T(128)} %param.29) | copy-start | bytes 196
  112.3 6.6 %copy-start.19 = (f32[4,16,16,64]{3,1,2,0:T(8,128)S(1)}, f32[4,16,16,64]{3,1,2,0:T(8,128)}, u32[]{:S(2)}) copy-start(f32[4,16,16,64]{3,1,2,0:T(8,128)} %convolution_bitcast_fusion.1) | copy-start | bytes 786436
Sparse Core Ops, SparseCore 0:
  9.9 89.7 all-gather.1
  105.8 28.5 reduce-scatter.1
where the time goes:
time: 143 us
  waiting for transfers between devices  72.3 us (51%)
  matrix products  26.1 us (18%)
  local copies, waits for them, and re-layouts  17.4 us (12%)
  between operations  14.5 us (10%)
  starting transfers between devices  8.85 us (6%)
  other arithmetic  3.73 us (3%)
    all_gather x1, waiting for transfers between devices, local(): lax.all_gather(w_out, 'rep', axis=1, tiled=True)  44.8 us
    all_to_all x1, waiting for transfers between devices, local(): lax.all_to_all(spread(home_pick, cache_own), 'rep', split_axis=0, concat_...  19 us
    dot_general x4, matrix products, spread(): mixed = jnp.dot(selector, flat, preferred_element_type=jnp.float32)  10.5 us
    reduce_scatter x1, waiting for transfers between devices, local(): lax.psum_scatter(terms, 'head', scatter_dimension=1, tiled=True)  7.77 us
    dot_general x1, matrix products, local(): jnp.dot(attn_flat, lax.all_gather(w_out, 'rep', axis=1, tiled=True), pref...  5.96 us
    all_to_all x1, starting transfers between devices, local(): lax.all_to_all(spread(home_pick, cache_own), 'rep', split_axis=0, concat_...  5.17 us
    dot_general x1, matrix products, scan_heads(): jnp.einsum('kue,kuen,kuep->kepn', weights_in, b_heads, signal, precision=...  4.74 us
    all_to_all x1, starting transfers between devices, local(): lax.all_to_all(spread(home_pick, ckpt_state), 'rep', split_axis=0, concat...  3.6 us
  transfers between devices with their start and end apart: 4, of which 3 were waited for; matrix products, arithmetic and copies ran while one was open for 32% of the time, Pallas kernels for 0%

commit v1 on v0

--- a/solution.py
+++ b/solution.py
@@ -1,8 +1,11 @@
+import functools
 import math
 
 import jax
 import jax.numpy as jnp
 from jax import lax
+from jax.experimental import pallas as pl
+from jax.experimental.pallas import tpu as pltpu
 from jax.sharding import PartitionSpec as P
 
 TAIL = 16
@@ -145,7 +148,9 @@
     ).astype(jnp.int32)
     slot_home = jnp.sum(holding, axis=1).T.astype(jnp.bfloat16)
     slot_pages = jnp.sum(holding[:, :, :, None] * page_grid[:, :, None, :], axis=(0, 1))
-    cache_own = kv_pool[slot_pages].reshape(slot_count, -1, kv_columns)
+    pool_range = jnp.arange(kv_pool.shape[0], dtype=jnp.int32)
+    page_pick = (slot_pages.reshape(-1, 1) == pool_range[None, :]).astype(jnp.bfloat16)
+    cache_own = spread(page_pick, kv_pool).reshape(slot_count, -1, kv_columns)
 
     def per_request(array):
         return array.reshape(slot_count, TAIL, -1)
@@ -206,9 +211,388 @@
     return (ssd_rows.reshape(slot_count * TAIL, -1), projected, final_rows)
 
 
+MESH = pl.DeviceIdType.MESH
+VMEM_BUDGET = 24 * 2**20
+
+
+def dot(a, b, dims=((1,), (0,)), precision=None):
+    return lax.dot_general(
+        a, b, (dims, ((), ())), precision=precision, preferred_element_type=jnp.float32
+    )
+
+
+def layer(
+    n,
+    m,
+    owner,
+    slot,
+    page,
+    hit,
+    tail,
+    x,
+    z,
+    b,
+    c,
+    dt,
+    q,
+    tkv,
+    ckpt,
+    pool,
+    w,
+    rate,
+    skip,
+    gain,
+    ssd_o,
+    proj_o,
+    fin_o,
+    kv_out,
+    kv_in,
+    st_out,
+    st_in,
+    rows_all,
+    part,
+    shares,
+    sums,
+    cum_s,
+    xw_s,
+    log_s,
+    acc_s,
+    kv_ss,
+    kv_rs,
+    st_ss,
+    st_rs,
+    rows_ss,
+    rows_rs,
+    part_ss,
+    part_rs,
+    sum_ss,
+    sum_rs,
+):
+    me = lax.axis_index("rep")
+    hd = lax.axis_index("head")
+    reqs = ckpt.shape[0]
+    heads = ckpt.shape[1]
+    size = ckpt.shape[2]
+    width = heads * size
+    pages = page.shape[1]
+    cache = pages * pool.shape[1]
+    span = n // m
+
+    def to_rep(s):
+        return lax.rem(me + s, n)
+
+    def from_rep(s):
+        return lax.rem(me + n - s, n)
+
+    barrier = pltpu.get_barrier_semaphore()
+    for s in range(1, n):
+        pl.semaphore_signal(
+            barrier, inc=1, device_id={"rep": to_rep(s)}, device_id_type=MESH
+        )
+    for u in range(1, m):
+        pl.semaphore_signal(
+            barrier, inc=1, device_id={"head": lax.rem(hd + u, m)}, device_id_type=MESH
+        )
+
+    def kv_copy(s):
+        return pltpu.make_async_remote_copy(
+            src_ref=kv_out.at[s],
+            dst_ref=kv_in.at[s],
+            send_sem=kv_ss.at[s],
+            recv_sem=kv_rs.at[s],
+            device_id={"rep": to_rep(s)},
+            device_id_type=MESH,
+        )
+
+    def st_copy(s):
+        return pltpu.make_async_remote_copy(
+            src_ref=st_out.at[s],
+            dst_ref=st_in.at[s],
+            send_sem=st_ss.at[s],
+            recv_sem=st_rs.at[s],
+            device_id={"rep": to_rep(s)},
+            device_id_type=MESH,
+        )
+
+    def rows_copy(s):
+        return pltpu.make_async_remote_copy(
+            src_ref=rows_all.at[0],
+            dst_ref=rows_all.at[s],
+            send_sem=rows_ss.at[s],
+            recv_sem=rows_rs.at[s],
+            device_id={"rep": to_rep(s)},
+            device_id_type=MESH,
+        )
+
+    def part_copy(s):
+        return pltpu.make_async_remote_copy(
+            src_ref=part.at[s],
+            dst_ref=shares.at[me],
+            send_sem=part_ss.at[s],
+            recv_sem=part_rs.at[s],
+            device_id={"rep": from_rep(s)},
+            device_id_type=MESH,
+        )
+
+    def sum_copy(u):
+        to = lax.rem(hd + u, m)
+        return pltpu.make_async_remote_copy(
+            src_ref=shares.at[pl.ds(to * span, span)],
+            dst_ref=sums.at[u],
+            send_sem=sum_ss.at[u],
+            recv_sem=sum_rs.at[u],
+            device_id={"head": to},
+            device_id_type=MESH,
+        )
+
+    def wanted(j):
+        request = j * reqs
+        for k in range(1, reqs):
+            request = jnp.where(owner[j * reqs + k] == me, j * reqs + k, request)
+        return request
+
+    def pack_pages(s, target):
+        request = wanted(to_rep(s))
+
+        def one(i, carry):
+            target[s, i] = pool[page[request, i]]
+            return carry
+
+        lax.fori_loop(0, pages, one, 0)
+
+    for s in range(1, n):
+        pack_pages(s, kv_out)
+        if s == 1:
+            pl.semaphore_wait(barrier, n - 1 + m - 1)
+        kv_copy(s).start()
+    pack_pages(0, kv_in)
+
+    def pack_state(s, target):
+        place = slot[wanted(to_rep(s))]
+
+        def one(e, carry):
+            target[s, e] = ckpt[place, e]
+            return carry
+
+        lax.fori_loop(0, heads, one, 0)
+
+    for s in range(1, n):
+        pack_state(s, st_out)
+        st_copy(s).start()
+    pack_state(0, st_in)
+
+    lane = lax.broadcasted_iota(jnp.int32, (heads, width), 1)
+    widen = (lane // size == lax.broadcasted_iota(jnp.int32, (heads, width), 0)).astype(
+        jnp.float32
+    )
+    count = reqs * TAIL
+    row = lax.broadcasted_iota(jnp.int32, (count, heads), 0)
+    live = jnp.zeros((count, heads), jnp.float32)
+    for k in range(reqs):
+        first = k * TAIL
+        live = jnp.where((row >= first) & (row < first + tail[me * reqs + k]), 1.0, live)
+    weighted = dt[...].astype(jnp.float32) * live
+    log_decay = -rate[...] * weighted
+    log_s[...] = log_decay
+    one_row = lax.broadcasted_iota(jnp.int32, (count, count), 0)
+    one_col = lax.broadcasted_iota(jnp.int32, (count, count), 1)
+    before = ((one_row >= one_col) & (one_row // TAIL == one_col // TAIL)).astype(jnp.float32)
+    cum = dot(before, log_decay, precision=highest)
+    cum_s[...] = dot(cum, widen, precision=highest)
+    xw_s[...] = dot(weighted, widen, precision=highest) * x[...].astype(jnp.float32)
+    skip_wide = dot(skip[...], widen, precision=highest)
+    step = lax.broadcasted_iota(jnp.int32, (TAIL, 1), 0)
+
+    def within(k, carry):
+        rows = pl.ds(pl.multiple_of(k * TAIL, TAIL), TAIL)
+        meet = dot(c[rows, :], b[rows, :], ((1,), (1,)))
+        running = cum_s[rows, :]
+        fed = xw_s[rows, :]
+        total = skip_wide * x[rows, :].astype(jnp.float32)
+        for u in range(TAIL):
+            seen = step >= u
+            decay = jnp.exp(jnp.where(seen, running - running[u : u + 1, :], 0.0))
+            factor = jnp.where(seen, meet[:, u : u + 1], 0.0)
+            total = total + decay * factor * fed[u : u + 1, :]
+        acc_s[rows, :] = total
+        return carry
+
+    lax.fori_loop(0, reqs, within, 0)
+
+    for s in range(1, n):
+        kv_copy(s).wait_recv()
+
+    scaling = 1.0 / math.sqrt(DH)
+
+    def attention(k, carry):
+        rows = pl.ds(pl.multiple_of(k * TAIL, TAIL), TAIL)
+        request = me * reqs + k
+        held = kv_in[lax.rem(me + n - owner[request], n)].reshape(cache, 2 * DH)
+        fresh = tkv[rows, :]
+        asked = jnp.concatenate(
+            [q[rows, a * DH : (a + 1) * DH] for a in range(QH_DEV)], axis=0
+        )
+        far = dot(asked, held[:, :DH], ((1,), (1,))) * scaling
+        near = dot(asked, fresh[:, :DH], ((1,), (1,))) * scaling
+        place = lax.broadcasted_iota(jnp.int32, far.shape, 1)
+        far_seen = place < hit[request]
+        at = lax.rem(lax.broadcasted_iota(jnp.int32, near.shape, 0), TAIL)
+        behind = lax.broadcasted_iota(jnp.int32, near.shape, 1)
+        near_seen = (behind <= at) & (behind < tail[request])
+        far = jnp.where(far_seen, far, -1e30)
+        near = jnp.where(near_seen, near, -1e30)
+        top = jnp.maximum(
+            jnp.max(far, axis=1, keepdims=True), jnp.max(near, axis=1, keepdims=True)
+        )
+        far = jnp.where(far_seen, jnp.exp(far - top), 0.0)
+        near = jnp.where(near_seen, jnp.exp(near - top), 0.0)
+        whole = jnp.sum(far, axis=1, keepdims=True) + jnp.sum(near, axis=1, keepdims=True)
+        far = (far / whole).astype(jnp.bfloat16)
+        near = (near / whole).astype(jnp.bfloat16)
+        result = dot(far, held[:, DH:]) + dot(near, fresh[:, DH:])
+        result = jnp.concatenate(
+            [result[a * TAIL : (a + 1) * TAIL, :] for a in range(QH_DEV)], axis=1
+        )
+        alive = (step < tail[request]).astype(jnp.float32)
+        rows_all[0, rows, :] = (result * alive).astype(jnp.bfloat16)
+        return carry
+
+    lax.fori_loop(0, reqs, attention, 0)
+    for s in range(1, n):
+        rows_copy(s).start()
+
+    for s in range(1, n):
+        st_copy(s).wait_recv()
+
+    def recur(k, carry):
+        rows = pl.ds(pl.multiple_of(k * TAIL, TAIL), TAIL)
+        request = me * reqs + k
+        start = st_in[lax.rem(me + n - owner[request], n)]
+        running = cum_s[rows, :]
+        carried = dot(c[rows, :], start.reshape(width, start.shape[2]), ((1,), (1,)))
+        alive = (step < tail[request]).astype(jnp.float32)
+        mixer = (acc_s[rows, :] + jnp.exp(running) * carried) * alive
+        gate = z[rows, :].astype(jnp.float32)
+        gated = mixer * (gate / (1.0 + jnp.exp(-gate)))
+        energy = jnp.sum(gated * gated, axis=1, keepdims=True)
+        normed = gated / jnp.sqrt(energy / width + 1e-05) * gain[...]
+        ssd_o[rows, :] = normed.astype(jnp.bfloat16)
+        fed = jnp.exp(running[TAIL - 1 : TAIL, :] - running) * xw_s[rows, :]
+        added = dot(fed, b[rows, :].astype(jnp.float32), ((0,), (0,)), precision=highest)
+        last = dot(
+            log_s[rows, :],
+            jnp.ones((TAIL, start.shape[2]), jnp.float32),
+            ((0,), (0,)),
+            precision=highest,
+        )
+        kept = jnp.exp(last)[:, None, :] * start.astype(jnp.float32)
+        fin_o[k] = (kept + added.reshape(start.shape)).astype(jnp.bfloat16)
+        return carry
+
+    lax.fori_loop(0, reqs, recur, 0)
+
+    shares[me] = dot(rows_all[0], w[...]).astype(jnp.bfloat16)
+    for s in range(1, n):
+        rows_copy(s).wait_recv()
+        part[s] = dot(rows_all[s], w[...]).astype(jnp.bfloat16)
+        part_copy(s).start()
+    for s in range(1, n):
+        pltpu.make_async_remote_copy(
+            src_ref=part.at[s],
+            dst_ref=shares.at[to_rep(s)],
+            send_sem=part_ss.at[s],
+            recv_sem=part_rs.at[s],
+            device_id={"rep": to_rep(s)},
+            device_id_type=MESH,
+        ).wait_recv()
+    for u in range(1, m):
+        sum_copy(u).start()
+    for u in range(1, m):
+        sum_copy(u).wait_recv()
+    columns = w.shape[1]
+    for j in range(span):
+        total = shares[hd * span + j].astype(jnp.float32)
+        for u in range(1, m):
+            total = total + sums[u, j].astype(jnp.float32)
+        proj_o[:, j * columns : (j + 1) * columns] = total.astype(jnp.bfloat16)
+
+    for s in range(1, n):
+        kv_copy(s).wait_send()
+        st_copy(s).wait_send()
+        rows_copy(s).wait_send()
+        part_copy(s).wait_send()
+    for u in range(1, m):
+        sum_copy(u).wait_send()
+
+
+def fused(n, m, *args):
+    ssd_x, gate_z, group_b, group_c, step_dt, queries, tail_kv, ckpt_state, kv_pool, w_out = args[:10]
+    decay_rate, skip_d, norm_gain, owner, slot, page_table, hit_len, tail_len = args[10:]
+    reqs, heads, size, state = ckpt_state.shape
+    count, width = ssd_x.shape
+    page_shape = (page_table.shape[1],) + kv_pool.shape[1:]
+    columns = w_out.shape[1]
+    bf16 = jnp.bfloat16
+    smem = pl.BlockSpec(memory_space=pltpu.SMEM)
+    vmem = pl.BlockSpec(memory_space=pltpu.VMEM)
+    scratch = [
+        pltpu.VMEM((n,) + page_shape, bf16),
+        pltpu.VMEM((n,) + page_shape, bf16),
+        pltpu.VMEM((n, heads, size, state), bf16),
+        pltpu.VMEM((n, heads, size, state), bf16),
+        pltpu.VMEM((n, count, queries.shape[1]), bf16),
+        pltpu.VMEM((n, count, columns), bf16),
+        pltpu.VMEM((n, count, columns), bf16),
+        pltpu.VMEM((m, n // m, count, columns), bf16),
+        pltpu.VMEM((count, width), jnp.float32),
+        pltpu.VMEM((count, width), jnp.float32),
+        pltpu.VMEM((count, heads), jnp.float32),
+        pltpu.VMEM((count, width), jnp.float32),
+    ] + [pltpu.SemaphoreType.DMA((k,)) for k in (n, n, n, n, n, n, n, n, m, m)]
+    return pl.pallas_call(
+        functools.partial(layer, n, m),
+        out_shape=(
+            jax.ShapeDtypeStruct((count, width), bf16),
+            jax.ShapeDtypeStruct((count, n // m * columns), bf16),
+            jax.ShapeDtypeStruct(ckpt_state.shape, bf16),
+        ),
+        in_specs=[smem] * 5 + [vmem] * 13,
+        out_specs=(vmem, vmem, vmem),
+        scratch_shapes=scratch,
+        compiler_params=pltpu.CompilerParams(
+            collective_id=0, has_side_effects=True, vmem_limit_bytes=2 * VMEM_BUDGET
+        ),
+    )(
+        owner,
+        slot,
+        page_table,
+        hit_len,
+        tail_len,
+        *args[:10],
+        decay_rate.reshape(1, -1),
+        skip_d.reshape(1, -1),
+        norm_gain.reshape(1, -1),
+    )
+
+
+def plan(n, m, *args):
+    ckpt_state, kv_pool, w_out, page_table = args[7], args[8], args[9], args[15]
+    state_bytes = 2 * math.prod(ckpt_state.shape[1:])
+    page_bytes = 2 * page_table.shape[1] * math.prod(kv_pool.shape[1:])
+    row_bytes = 2 * args[0].shape[0] * (args[5].shape[1] + 3 * w_out.shape[1])
+    held = 2 * (2 * ckpt_state.size + kv_pool.size + w_out.size)
+    need = n * (2 * state_bytes + 2 * page_bytes + row_bytes) + held
+    one_group = (
+        args[6].shape[1] == 2 * DH and args[2].shape[1] == STATE and args[5].shape[1] == QH_DEV * DH
+    )
+    if need <= VMEM_BUDGET and one_group and n % m == 0:
+        return fused(n, m, *args)
+    return local(*args)
+
+
 def solution(mesh):
     return jax.shard_map(
-        local,
+        functools.partial(plan, mesh.shape["rep"], mesh.shape["head"]),
         mesh=mesh,
         in_specs=(
             P("rep", "head"),

time: 143 us -> 85.5 us (0.60)
  waiting for transfers between devices: 72.3 us -> 0 us
  Pallas kernels: 0 us -> 70.8 us
  matrix products: 26.1 us -> 0 us
  between operations: 14.5 us -> 0.72 us
  starting transfers between devices: 8.85 us -> 0 us
  local copies, waits for them, and re-layouts: 17.4 us -> 13.5 us
  other arithmetic: 3.73 us -> 0 us
    pallas_call x0 -> x1, Pallas kernels: none -> 70.8 us  [fused(): pl.pallas_call(functools.partial(layer, n, m), out_shape=(jax.ShapeDtypeS...]
    all_gather x1 -> x0, waiting for transfers between devices: 44.8 us -> none  [local(): lax.all_gather(w_out, 'rep', axis=1, tiled=True)]
    dot_general x13 -> x0, matrix products: 26.1 us -> none  [the longest x4 10.5 us: spread(): mixed = jnp.dot(selector, flat, preferred_element_type=jnp.float32)]
    all_to_all x2 -> x0, waiting for transfers between devices: 19 us -> none  [the longest x1 19 us: local(): lax.all_to_all(spread(home_pick, cache_own), 'rep', split_axis=0, concat_...]
    unnamed x44 -> x37, local copies, waits for them, and re-layouts: 3.19 us -> 13.5 us
    all_to_all x2 -> x0, starting transfers between devices: 8.77 us -> none  [the longest x1 5.17 us: local(): lax.all_to_all(spread(home_pick, cache_own), 'rep', split_axis=0, concat_...]
    reduce_scatter x1 -> x0, waiting for transfers between devices: 7.77 us -> none  [local(): lax.psum_scatter(terms, 'head', scatter_dimension=1, tiled=True)]
    reshape x5 -> x0, local copies, waits for them, and re-layouts: 3.98 us -> none  [the longest x2 3.09 us: spread(): mixed.astype(values.dtype).reshape((selector.shape[0],) + values.shape[1:])]
  transfers between devices with their start and end apart: 4 -> 0, of which waited for: 3 -> 0; matrix products, arithmetic and copies ran while one was open for 32% -> 0% of each run, Pallas kernels for 0% -> 0%
where the time goes in v1:
time: 85.5 us; the launch traced here: 84.9 us
  Pallas kernels  70.8 us (83%)
  local copies, waits for them, and re-layouts  13.5 us (16%)
    pallas_call x1, Pallas kernels, fused(): pl.pallas_call(functools.partial(layer, n, m), out_shape=(jax.ShapeDtypeS...  70.8 us
    unnamed x37, local copies, waits for them, and re-layouts  13.5 us

profile of v1, /device:TPU:0, one launch (start us, length us, event | category | flops | bytes accessed | tf_op | source)
XLA Modules:
  0.0 84.9 jit_solution(1351761098020865175)
XLA Ops:
  0.6 0.0 copy-start.6
  0.6 0.8 copy.22.dt
  1.4 0.0 copy-start.10
  1.4 0.0 copy-start.11
  1.5 0.0 copy-start.12
  1.5 0.8 copy.21.page
  2.3 0.0 copy-done.6
  2.3 0.0 copy-done.7
  2.3 0.0 copy-start
  2.3 1.2 %copy-done = bf16[4,16,64,128]{3,2,1,0:T(8,128)(2,1)S(1)} copy-done((bf16[4,16,64,128]{3,2,1,0:T(8,128)(2,1)S(1)}, bf16[4,16,64,128]{3,2,1,0:T(8,128)(2,1)}, u32[]{:S(2)}) %copy-start) | copy-done | bytes 1048600
  3.5 1.2 %copy-done.1 = bf16[1024,512]{1,0:T(8,128)(2,1)S(1)} copy-done((bf16[1024,512]{1,0:T(8,128)(2,1)S(1)}, bf16[1024,512]{1,0:T(8,128)(2,1)}, u32[]{:S(2)}) %copy-start.1) | copy-done | bytes 1048600
  4.8 1.0 %copy-done.2 = bf16[64,16,256]{2,1,0:T(8,128)(2,1)S(1)} copy-done((bf16[64,16,256]{2,1,0:T(8,128)(2,1)S(1)}, bf16[64,16,256]{2,1,0:T(8,128)(2,1)}, u32[]{:S(2)}) %copy-start.2) | copy-done | bytes 524312
  5.8 0.9 %copy-done.3 = bf16[64,1024]{1,0:T(8,128)(2,1)S(1)} copy-done((bf16[64,1024]{1,0:T(8,128)(2,1)S(1)}, bf16[64,1024]{1,0:T(8,128)(2,1)}, u32[]{:S(2)}) %copy-start.3) | copy-done | bytes 131096
  6.7 0.9 %copy-done.4 = bf16[64,1024]{1,0:T(8,128)(2,1)S(1)} copy-done((bf16[64,1024]{1,0:T(8,128)(2,1)S(1)}, bf16[64,1024]{1,0:T(8,128)(2,1)}, u32[]{:S(2)}) %copy-start.4) | copy-done | bytes 131096
  7.6 0.9 %copy-done.5 = bf16[64,1024]{1,0:T(8,128)(2,1)S(1)} copy-done((bf16[64,1024]{1,0:T(8,128)(2,1)S(1)}, bf16[64,1024]{1,0:T(8,128)(2,1)}, u32[]{:S(2)}) %copy-start.5) | copy-done | bytes 131096
  8.5 0.7 copy-done.8
  9.2 0.7 copy-done.9
  9.9 0.7 copy-done.13
  10.6 0.7 copy-done.14
  11.2 0.7 copy-done.15
  11.9 70.8 %shard_map.193 = (bf16[64,1024]{1,0:T(8,128)(2,1)S(1)}, bf16[64,1024]{1,0:T(8,128)(2,1)S(1)}, bf16[4,16,64,128]{3,2,1,0:T(8,128)(2,1)S(1)}) custom-call(s32[32]{0:T(128)S(1)} %copy-done.10, s32[32]{0:T(128)S(1)} %copy-done.11, s32[32,16]{1,0:T(8,128)S(1)} %copy.21.page, s32[32]{0:T(128)S(1)} %copy-done.12, s32[32]{0:T(128)S(1)} %copy-done.13, ...), custom_call_target="tpu_custom_call" | custom-call | tf_op jit(solution)/shard_map/pallas_call | solution.py:552
  82.6 0.7 copy.26
  83.3 0.7 copy.27
  84.0 1.0 %copy.28 = bf16[4,16,64,128]{3,2,1,0:T(8,128)(2,1)} copy(bf16[4,16,64,128]{3,2,1,0:T(8,128)(2,1)S(1)} %get-tuple-element.8) | data formatting | bytes 2097152
  (14 shorter events, 0.0 us)
Async XLA Ops:
  0.6 1.6 %copy-start.6 = (bf16[64,256]{1,0:T(8,128)(2,1)S(1)}, bf16[64,256]{1,0:T(8,128)(2,1)}, u32[]{:S(2)}) copy-start(bf16[64,256]{1,0:T(8,128)(2,1)} %tkv.1) | copy-start | bytes 98308
  1.4 0.8 copy-start.7
  1.4 0.8 copy-start.10
  1.4 0.8 copy-start.11
  1.5 0.8 copy-start.12
  2.3 1.2 %copy-start = (bf16[4,16,64,128]{3,2,1,0:T(8,128)(2,1)S(1)}, bf16[4,16,64,128]{3,2,1,0:T(8,128)(2,1)}, u32[]{:S(2)}) copy-start(bf16[4,16,64,128]{3,2,1,0:T(8,128)(2,1)} %ckpt.1) | copy-start | bytes 3145732
  3.5 1.2 %copy-start.1 = (bf16[1024,512]{1,0:T(8,128)(2,1)S(1)}, bf16[1024,512]{1,0:T(8,128)(2,1)}, u32[]{:S(2)}) copy-start(bf16[1024,512]{1,0:T(8,128)(2,1)} %w.1) | copy-start | bytes 3145732
  4.8 1.0 %copy-start.2 = (bf16[64,16,256]{2,1,0:T(8,128)(2,1)S(1)}, bf16[64,16,256]{2,1,0:T(8,128)(2,1)}, u32[]{:S(2)}) copy-start(bf16[64,16,256]{2,1,0:T(8,128)(2,1)} %pool.1) | copy-start | bytes 1572868
  5.8 0.9 %copy-start.3 = (bf16[64,1024]{1,0:T(8,128)(2,1)S(1)}, bf16[64,1024]{1,0:T(8,128)(2,1)}, u32[]{:S(2)}) copy-start(bf16[64,1024]{1,0:T(8,128)(2,1)} %x.1) | copy-start | bytes 393220
  6.7 0.9 %copy-start.4 = (bf16[64,1024]{1,0:T(8,128)(2,1)S(1)}, bf16[64,1024]{1,0:T(8,128)(2,1)}, u32[]{:S(2)}) copy-start(bf16[64,1024]{1,0:T(8,128)(2,1)} %z.1) | copy-start | bytes 393220
  7.6 0.9 %copy-start.5 = (bf16[64,1024]{1,0:T(8,128)(2,1)S(1)}, bf16[64,1024]{1,0:T(8,128)(2,1)}, u32[]{:S(2)}) copy-start(bf16[64,1024]{1,0:T(8,128)(2,1)} %q.1) | copy-start | bytes 393220
  8.5 0.7 copy-start.8
  9.2 0.7 copy-start.9
  9.9 0.7 copy-start.13
  10.6 0.7 copy-start.14
  11.2 0.7 copy-start.15

commit v2 on v1

--- a/solution.py
+++ b/solution.py
@@ -224,6 +224,27 @@
 def layer(
     n,
     m,
+    owner_h,
+    slot_h,
+    page_h,
+    hit_h,
+    tail_h,
+    x_h,
+    z_h,
+    b_h,
+    c_h,
+    dt_h,
+    q_h,
+    tkv_h,
+    ckpt_h,
+    pool_h,
+    w_h,
+    rate_h,
+    skip_h,
+    gain_h,
+    ssd_o,
+    proj_o,
+    fin_o,
     owner,
     slot,
     page,
@@ -242,9 +263,6 @@
     rate,
     skip,
     gain,
-    ssd_o,
-    proj_o,
-    fin_o,
     kv_out,
     kv_in,
     st_out,
@@ -267,6 +285,9 @@
     part_rs,
     sum_ss,
     sum_rs,
+    in_sem,
+    w_ss,
+    w_rs,
 ):
     me = lax.axis_index("rep")
     hd = lax.axis_index("head")
@@ -277,6 +298,20 @@
     pages = page.shape[1]
     cache = pages * pool.shape[1]
     span = n // m
+    chips = n // 2
+    core = lax.rem(me, 2)
+    twin = me + 1 - 2 * core
+    chip_first = me - core
+    sources = (owner_h, slot_h, page_h, hit_h, tail_h, pool_h, ckpt_h, dt_h, rate_h, skip_h)
+    sources += (x_h, b_h, c_h, q_h, tkv_h, z_h, gain_h, w_h)
+    targets = (owner, slot, page, hit, tail, pool, ckpt, dt, rate, skip)
+    targets += (x, b, c, q, tkv, z, gain, w.at[core])
+    loads = [
+        pltpu.make_async_copy(source, target, in_sem.at[i])
+        for i, (source, target) in enumerate(zip(sources, targets))
+    ]
+    for load in loads:
+        load.start()
 
     def to_rep(s):
         return lax.rem(me + s, n)
@@ -314,23 +349,33 @@
             device_id_type=MESH,
         )
 
+    def w_copy():
+        return pltpu.make_async_remote_copy(
+            src_ref=w_h,
+            dst_ref=w.at[core],
+            send_sem=w_ss,
+            recv_sem=w_rs,
+            device_id={"rep": twin},
+            device_id_type=MESH,
+        )
+
     def rows_copy(s):
         return pltpu.make_async_remote_copy(
             src_ref=rows_all.at[0],
             dst_ref=rows_all.at[s],
             send_sem=rows_ss.at[s],
             recv_sem=rows_rs.at[s],
-            device_id={"rep": to_rep(s)},
+            device_id={"rep": to_rep(2 * s)},
             device_id_type=MESH,
         )
 
     def part_copy(s):
         return pltpu.make_async_remote_copy(
             src_ref=part.at[s],
-            dst_ref=shares.at[me],
+            dst_ref=shares.at[pl.ds(chip_first, 2)],
             send_sem=part_ss.at[s],
             recv_sem=part_rs.at[s],
-            device_id={"rep": from_rep(s)},
+            device_id={"rep": from_rep(2 * s)},
             device_id_type=MESH,
         )
 
@@ -360,6 +405,8 @@
 
         lax.fori_loop(0, pages, one, 0)
 
+    for load in loads[:6]:
+        load.wait()
     for s in range(1, n):
         pack_pages(s, kv_out)
         if s == 1:
@@ -376,10 +423,17 @@
 
         lax.fori_loop(0, heads, one, 0)
 
-    for s in range(1, n):
+    early = chips - 1
+    loads[6].wait()
+    for s in range(1, early + 1):
         pack_state(s, st_out)
         st_copy(s).start()
+    w_copy().start()
     pack_state(0, st_in)
+    for s in range(early + 1, n):
+        pack_state(s, st_out)
+    for load in loads[7:]:
+        load.wait()
 
     lane = lax.broadcasted_iota(jnp.int32, (heads, width), 1)
     widen = (lane // size == lax.broadcasted_iota(jnp.int32, (heads, width), 0)).astype(
@@ -458,11 +512,10 @@
         return carry
 
     lax.fori_loop(0, reqs, attention, 0)
-    for s in range(1, n):
+    for s in range(1, chips):
         rows_copy(s).start()
-
-    for s in range(1, n):
-        st_copy(s).wait_recv()
+    for s in range(early + 1, n):
+        st_copy(s).start()
 
     def recur(k, carry):
         rows = pl.ds(pl.multiple_of(k * TAIL, TAIL), TAIL)
@@ -489,27 +542,41 @@
         fin_o[k] = (kept + added.reshape(start.shape)).astype(jnp.bfloat16)
         return carry
 
-    lax.fori_loop(0, reqs, recur, 0)
-
-    shares[me] = dot(rows_all[0], w[...]).astype(jnp.bfloat16)
-    for s in range(1, n):
+    pltpu.make_async_remote_copy(
+        src_ref=w_h,
+        dst_ref=w.at[1 - core],
+        send_sem=w_ss,
+        recv_sem=w_rs,
+        device_id={"rep": twin},
+        device_id_type=MESH,
+    ).wait_recv()
+    for i in range(2):
+        shares[chip_first + i] = dot(rows_all[0], w[i]).astype(jnp.bfloat16)
+    for s in range(1, chips):
         rows_copy(s).wait_recv()
-        part[s] = dot(rows_all[s], w[...]).astype(jnp.bfloat16)
+        for i in range(2):
+            part[s, i] = dot(rows_all[s], w[i]).astype(jnp.bfloat16)
         part_copy(s).start()
-    for s in range(1, n):
+    for s in range(1, chips):
+        peer = to_rep(2 * s)
         pltpu.make_async_remote_copy(
             src_ref=part.at[s],
-            dst_ref=shares.at[to_rep(s)],
+            dst_ref=shares.at[pl.ds(peer - core, 2)],
             send_sem=part_ss.at[s],
             recv_sem=part_rs.at[s],
-            device_id={"rep": to_rep(s)},
+            device_id={"rep": peer},
             device_id_type=MESH,
         ).wait_recv()
     for u in range(1, m):
         sum_copy(u).start()
+
+    for s in range(1, n):
+        st_copy(s).wait_recv()
+    lax.fori_loop(0, reqs, recur, 0)
+
     for u in range(1, m):
         sum_copy(u).wait_recv()
-    columns = w.shape[1]
+    columns = w.shape[2]
     for j in range(span):
         total = shares[hd * span + j].astype(jnp.float32)
         for u in range(1, m):
@@ -519,8 +586,10 @@
     for s in range(1, n):
         kv_copy(s).wait_send()
         st_copy(s).wait_send()
+    for s in range(1, chips):
         rows_copy(s).wait_send()
         part_copy(s).wait_send()
+    w_copy().wait_send()
     for u in range(1, m):
         sum_copy(u).wait_send()
 
@@ -533,22 +602,29 @@
     page_shape = (page_table.shape[1],) + kv_pool.shape[1:]
     columns = w_out.shape[1]
     bf16 = jnp.bfloat16
-    smem = pl.BlockSpec(memory_space=pltpu.SMEM)
+    hbm = pl.BlockSpec(memory_space=pltpu.HBM)
     vmem = pl.BlockSpec(memory_space=pltpu.VMEM)
-    scratch = [
+    params = [p.reshape(1, -1) for p in (decay_rate, skip_d, norm_gain)]
+    operands = (owner, slot, page_table, hit_len, tail_len, *args[:10], *params)
+    scratch = [pltpu.SMEM(p.shape, p.dtype) for p in operands[:5]]
+    scratch += [pltpu.VMEM(p.shape, p.dtype) for p in operands[5:14]]
+    scratch += [pltpu.VMEM((2,) + w_out.shape, bf16)]
+    scratch += [pltpu.VMEM(p.shape, p.dtype) for p in params]
+    scratch += [
         pltpu.VMEM((n,) + page_shape, bf16),
         pltpu.VMEM((n,) + page_shape, bf16),
         pltpu.VMEM((n, heads, size, state), bf16),
         pltpu.VMEM((n, heads, size, state), bf16),
-        pltpu.VMEM((n, count, queries.shape[1]), bf16),
-        pltpu.VMEM((n, count, columns), bf16),
+        pltpu.VMEM((n // 2, count, queries.shape[1]), bf16),
+        pltpu.VMEM((n // 2, 2, count, columns), bf16),
         pltpu.VMEM((n, count, columns), bf16),
         pltpu.VMEM((m, n // m, count, columns), bf16),
         pltpu.VMEM((count, width), jnp.float32),
         pltpu.VMEM((count, width), jnp.float32),
         pltpu.VMEM((count, heads), jnp.float32),
         pltpu.VMEM((count, width), jnp.float32),
-    ] + [pltpu.SemaphoreType.DMA((k,)) for k in (n, n, n, n, n, n, n, n, m, m)]
+    ] + [pltpu.SemaphoreType.DMA((k,)) for k in (n, n, n, n, n, n, n, n, m, m, 18)]
+    scratch += [pltpu.SemaphoreType.DMA, pltpu.SemaphoreType.DMA]
     return pl.pallas_call(
         functools.partial(layer, n, m),
         out_shape=(
@@ -556,23 +632,13 @@
             jax.ShapeDtypeStruct((count, n // m * columns), bf16),
             jax.ShapeDtypeStruct(ckpt_state.shape, bf16),
         ),
-        in_specs=[smem] * 5 + [vmem] * 13,
+        in_specs=[hbm] * 18,
         out_specs=(vmem, vmem, vmem),
         scratch_shapes=scratch,
         compiler_params=pltpu.CompilerParams(
             collective_id=0, has_side_effects=True, vmem_limit_bytes=2 * VMEM_BUDGET
         ),
-    )(
-        owner,
-        slot,
-        page_table,
-        hit_len,
-        tail_len,
-        *args[:10],
-        decay_rate.reshape(1, -1),
-        skip_d.reshape(1, -1),
-        norm_gain.reshape(1, -1),
-    )
+    )(*operands)
 
 
 def plan(n, m, *args):
@@ -580,12 +646,12 @@
     state_bytes = 2 * math.prod(ckpt_state.shape[1:])
     page_bytes = 2 * page_table.shape[1] * math.prod(kv_pool.shape[1:])
     row_bytes = 2 * args[0].shape[0] * (args[5].shape[1] + 3 * w_out.shape[1])
-    held = 2 * (2 * ckpt_state.size + kv_pool.size + w_out.size)
+    held = 2 * (2 * ckpt_state.size + kv_pool.size + 2 * w_out.size)
     need = n * (2 * state_bytes + 2 * page_bytes + row_bytes) + held
     one_group = (
         args[6].shape[1] == 2 * DH and args[2].shape[1] == STATE and args[5].shape[1] == QH_DEV * DH
     )
-    if need <= VMEM_BUDGET and one_group and n % m == 0:
+    if need <= VMEM_BUDGET and one_group and n % m == 0 and n % 2 == 0:
         return fused(n, m, *args)
     return local(*args)
 

time: 85.5 us -> 79.6 us (0.931)
  Pallas kernels: 70.8 us -> 64.9 us
    pallas_call x1, Pallas kernels: 70.8 us -> 64.9 us  [fused(): pl.pallas_call(functools.partial(layer, n, m), out_shape=(jax.ShapeDtypeS...]
where the time goes in v2:
time: 79.6 us; the launch traced here: 79.1 us
  Pallas kernels  64.9 us (82%)
  local copies, waits for them, and re-layouts  13.5 us (17%)
    pallas_call x1, Pallas kernels, fused(): pl.pallas_call(functools.partial(layer, n, m), out_shape=(jax.ShapeDtypeS...  64.9 us
    unnamed x37, local copies, waits for them, and re-layouts  13.5 us

profile of v2, /device:TPU:0, one launch (start us, length us, event | category | flops | bytes accessed | tf_op | source)
XLA Modules:
  0.0 79.1 jit_solution(9539092442130509373)
XLA Ops:
  0.6 0.0 copy-start.6
  0.6 0.8 copy.22.dt_h
  1.4 0.0 copy-start.10
  1.4 0.0 copy-start.11
  1.5 0.0 copy-start.12
  1.5 0.8 %copy.21.page_h = s32[32,16]{1,0:T(8,128)S(1)} copy(s32[32,16]{0,1:T(8,128)} %param.33) | data formatting | bytes 4096 | tf_op args[15]
  2.3 0.0 copy-done.6
  2.3 0.0 copy-done.7
  2.3 0.0 copy-start
  2.3 1.2 %copy-done = bf16[4,16,64,128]{3,2,1,0:T(8,128)(2,1)S(1)} copy-done((bf16[4,16,64,128]{3,2,1,0:T(8,128)(2,1)S(1)}, bf16[4,16,64,128]{3,2,1,0:T(8,128)(2,1)}, u32[]{:S(2)}) %copy-start) | copy-done | bytes 1048600
  3.5 1.2 %copy-done.1 = bf16[1024,512]{1,0:T(8,128)(2,1)S(1)} copy-done((bf16[1024,512]{1,0:T(8,128)(2,1)S(1)}, bf16[1024,512]{1,0:T(8,128)(2,1)}, u32[]{:S(2)}) %copy-start.1) | copy-done | bytes 1048600
  4.8 1.0 %copy-done.2 = bf16[64,16,256]{2,1,0:T(8,128)(2,1)S(1)} copy-done((bf16[64,16,256]{2,1,0:T(8,128)(2,1)S(1)}, bf16[64,16,256]{2,1,0:T(8,128)(2,1)}, u32[]{:S(2)}) %copy-start.2) | copy-done | bytes 524312
  5.8 0.9 %copy-done.3 = bf16[64,1024]{1,0:T(8,128)(2,1)S(1)} copy-done((bf16[64,1024]{1,0:T(8,128)(2,1)S(1)}, bf16[64,1024]{1,0:T(8,128)(2,1)}, u32[]{:S(2)}) %copy-start.3) | copy-done | bytes 131096
  6.7 0.9 %copy-done.4 = bf16[64,1024]{1,0:T(8,128)(2,1)S(1)} copy-done((bf16[64,1024]{1,0:T(8,128)(2,1)S(1)}, bf16[64,1024]{1,0:T(8,128)(2,1)}, u32[]{:S(2)}) %copy-start.4) | copy-done | bytes 131096
  7.6 0.9 %copy-done.5 = bf16[64,1024]{1,0:T(8,128)(2,1)S(1)} copy-done((bf16[64,1024]{1,0:T(8,128)(2,1)S(1)}, bf16[64,1024]{1,0:T(8,128)(2,1)}, u32[]{:S(2)}) %copy-start.5) | copy-done | bytes 131096
  8.5 0.7 copy-done.8
  9.2 0.7 copy-done.9
  9.9 0.7 copy-done.13
  10.6 0.7 copy-done.14
  11.2 0.7 copy-done.15
  11.9 64.9 %shard_map.193 = (bf16[64,1024]{1,0:T(8,128)(2,1)S(1)}, bf16[64,1024]{1,0:T(8,128)(2,1)S(1)}, bf16[4,16,64,128]{3,2,1,0:T(8,128)(2,1)S(1)}) custom-call(s32[32]{0:T(128)S(1)} %copy-done.10, s32[32]{0:T(128)S(1)} %copy-done.11, s32[32,16]{1,0:T(8,128)S(1)} %copy.21.page_h, s32[32]{0:T(128)S(1)} %copy-done.12, s32[32]{0:T(128)S(1)} %copy-done.13, ...), custom_call_target="tpu_custom_call" | custom-call | tf_op jit(solution)/shard_map/pallas_call | solution.py:628
  76.8 0.7 copy.26
  77.4 0.7 copy.27
  78.1 1.0 %copy.28 = bf16[4,16,64,128]{3,2,1,0:T(8,128)(2,1)} copy(bf16[4,16,64,128]{3,2,1,0:T(8,128)(2,1)S(1)} %get-tuple-element.8) | data formatting | bytes 2097152
  (14 shorter events, 0.0 us)
Async XLA Ops:
  0.6 1.6 %copy-start.6 = (bf16[64,256]{1,0:T(8,128)(2,1)S(1)}, bf16[64,256]{1,0:T(8,128)(2,1)}, u32[]{:S(2)}) copy-start(bf16[64,256]{1,0:T(8,128)(2,1)} %tkv_h.1) | copy-start | bytes 98308
  1.4 0.8 %copy-start.7 = (bf16[64,128]{1,0:T(8,128)(2,1)S(1)}, bf16[64,128]{1,0:T(8,128)(2,1)}, u32[]{:S(2)}) copy-start(bf16[64,128]{1,0:T(8,128)(2,1)} %b_h.1) | copy-start | bytes 49156
  1.4 0.8 %copy-start.10 = (s32[32]{0:T(128)S(1)}, s32[32]{0:T(128)}, u32[]{:S(2)}) copy-start(s32[32]{0:T(128)} %owner_h.1) | copy-start | bytes 388
  1.4 0.8 %copy-start.11 = (s32[32]{0:T(128)S(1)}, s32[32]{0:T(128)}, u32[]{:S(2)}) copy-start(s32[32]{0:T(128)} %slot_h.1) | copy-start | bytes 388
  1.5 0.8 %copy-start.12 = (s32[32]{0:T(128)S(1)}, s32[32]{0:T(128)}, u32[]{:S(2)}) copy-start(s32[32]{0:T(128)} %hit_h.1) | copy-start | bytes 388
  2.3 1.2 %copy-start = (bf16[4,16,64,128]{3,2,1,0:T(8,128)(2,1)S(1)}, bf16[4,16,64,128]{3,2,1,0:T(8,128)(2,1)}, u32[]{:S(2)}) copy-start(bf16[4,16,64,128]{3,2,1,0:T(8,128)(2,1)} %ckpt_h.1) | copy-start | bytes 3145732
  3.5 1.2 %copy-start.1 = (bf16[1024,512]{1,0:T(8,128)(2,1)S(1)}, bf16[1024,512]{1,0:T(8,128)(2,1)}, u32[]{:S(2)}) copy-start(bf16[1024,512]{1,0:T(8,128)(2,1)} %w_h.1) | copy-start | bytes 3145732
  4.8 1.0 %copy-start.2 = (bf16[64,16,256]{2,1,0:T(8,128)(2,1)S(1)}, bf16[64,16,256]{2,1,0:T(8,128)(2,1)}, u32[]{:S(2)}) copy-start(bf16[64,16,256]{2,1,0:T(8,128)(2,1)} %pool_h.1) | copy-start | bytes 1572868
  5.8 0.9 %copy-start.3 = (bf16[64,1024]{1,0:T(8,128)(2,1)S(1)}, bf16[64,1024]{1,0:T(8,128)(2,1)}, u32[]{:S(2)}) copy-start(bf16[64,1024]{1,0:T(8,128)(2,1)} %x_h.1) | copy-start | bytes 393220
  6.7 0.9 %copy-start.4 = (bf16[64,1024]{1,0:T(8,128)(2,1)S(1)}, bf16[64,1024]{1,0:T(8,128)(2,1)}, u32[]{:S(2)}) copy-start(bf16[64,1024]{1,0:T(8,128)(2,1)} %z_h.1) | copy-start | bytes 393220
  7.6 0.9 %copy-start.5 = (bf16[64,1024]{1,0:T(8,128)(2,1)S(1)}, bf16[64,1024]{1,0:T(8,128)(2,1)}, u32[]{:S(2)}) copy-start(bf16[64,1024]{1,0:T(8,128)(2,1)} %q_h.1) | copy-start | bytes 393220
  8.5 0.7 copy-start.8
  9.2 0.7 copy-start.9
  9.9 0.7 copy-start.13
  10.6 0.7 copy-start.14
  11.2 0.7 copy-start.15

commit v3 on v2

--- a/solution.py
+++ b/solution.py
@@ -1,4 +1,5 @@
 import functools
+import itertools
 import math
 
 import jax
@@ -213,6 +214,8 @@
 
 MESH = pl.DeviceIdType.MESH
 VMEM_BUDGET = 24 * 2**20
+SHARES = (1, 2, 2, 2)
+VMEM_LIMIT = 62 * 2**20
 
 
 def dot(a, b, dims=((1,), (0,)), precision=None):
@@ -295,7 +298,7 @@
     heads = ckpt.shape[1]
     size = ckpt.shape[2]
     width = heads * size
-    pages = page.shape[1]
+    pages = page.shape[0]
     cache = pages * pool.shape[1]
     span = n // m
     chips = n // 2
@@ -400,7 +403,7 @@
         request = wanted(to_rep(s))
 
         def one(i, carry):
-            target[s, i] = pool[page[request, i]]
+            target[s, i] = pool[page[i, request]]
             return carry
 
         lax.fori_loop(0, pages, one, 0)
@@ -423,14 +426,17 @@
 
         lax.fori_loop(0, heads, one, 0)
 
-    early = chips - 1
+    stops = [(n - 1) * k // sum(SHARES) for k in itertools.accumulate(SHARES)]
+    first, second, third, fourth = (
+        range(1 + begin, 1 + end) for begin, end in zip([0] + stops, stops)
+    )
     loads[6].wait()
-    for s in range(1, early + 1):
+    for s in first:
         pack_state(s, st_out)
         st_copy(s).start()
     w_copy().start()
     pack_state(0, st_in)
-    for s in range(early + 1, n):
+    for s in range(1 + stops[0], n):
         pack_state(s, st_out)
     for load in loads[7:]:
         load.wait()
@@ -445,7 +451,11 @@
     for k in range(reqs):
         first = k * TAIL
         live = jnp.where((row >= first) & (row < first + tail[me * reqs + k]), 1.0, live)
-    weighted = dt[...].astype(jnp.float32) * live
+    same = lax.broadcasted_iota(jnp.int32, (heads, heads), 0) == lax.broadcasted_iota(
+        jnp.int32, (heads, heads), 1
+    )
+    steps = dot(dt[...].astype(jnp.float32), same.astype(jnp.float32), ((0,), (0,)), highest)
+    weighted = steps * live
     log_decay = -rate[...] * weighted
     log_s[...] = log_decay
     one_row = lax.broadcasted_iota(jnp.int32, (count, count), 0)
@@ -514,7 +524,7 @@
     lax.fori_loop(0, reqs, attention, 0)
     for s in range(1, chips):
         rows_copy(s).start()
-    for s in range(early + 1, n):
+    for s in second:
         st_copy(s).start()
 
     def recur(k, carry):
@@ -557,6 +567,8 @@
         for i in range(2):
             part[s, i] = dot(rows_all[s], w[i]).astype(jnp.bfloat16)
         part_copy(s).start()
+    for s in third:
+        st_copy(s).start()
     for s in range(1, chips):
         peer = to_rep(2 * s)
         pltpu.make_async_remote_copy(
@@ -569,6 +581,8 @@
         ).wait_recv()
     for u in range(1, m):
         sum_copy(u).start()
+    for s in fourth:
+        st_copy(s).start()
 
     for s in range(1, n):
         st_copy(s).wait_recv()
@@ -605,7 +619,8 @@
     hbm = pl.BlockSpec(memory_space=pltpu.HBM)
     vmem = pl.BlockSpec(memory_space=pltpu.VMEM)
     params = [p.reshape(1, -1) for p in (decay_rate, skip_d, norm_gain)]
-    operands = (owner, slot, page_table, hit_len, tail_len, *args[:10], *params)
+    operands = (owner, slot, page_table.T, hit_len, tail_len)
+    operands += (*args[:4], step_dt.T, *args[5:10], *params)
     scratch = [pltpu.SMEM(p.shape, p.dtype) for p in operands[:5]]
     scratch += [pltpu.VMEM(p.shape, p.dtype) for p in operands[5:14]]
     scratch += [pltpu.VMEM((2,) + w_out.shape, bf16)]
@@ -636,7 +651,7 @@
         out_specs=(vmem, vmem, vmem),
         scratch_shapes=scratch,
         compiler_params=pltpu.CompilerParams(
-            collective_id=0, has_side_effects=True, vmem_limit_bytes=2 * VMEM_BUDGET
+            collective_id=0, has_side_effects=True, vmem_limit_bytes=VMEM_LIMIT
         ),
     )(*operands)
 

time: 79.6 us -> 64 us (0.80)
  the two profiles are of different devices: /device:TPU:0 before, /device:TPU:3 now
where the time goes in v3:
time: 64 us; the launch traced here: 63.8 us
  Pallas kernels  58.7 us (92%)
  local copies, waits for them, and re-layouts  4.52 us (7%)
  between operations  0.66 us (1%)
    pallas_call x1, Pallas kernels, fused(): pl.pallas_call(functools.partial(layer, n, m), out_shape=(jax.ShapeDtypeS...  58.7 us
    unnamed x5, local copies, waits for them, and re-layouts  4.52 us

profile of v3, /device:TPU:3, one launch (start us, length us, event | category | flops | bytes accessed | tf_op | source)
XLA Modules:
  0.0 63.8 jit_solution(327105062127201888)
XLA Ops:
  0.6 58.7 %shard_map.193 = (bf16[64,1024]{1,0:T(8,128)(2,1)}, bf16[64,1024]{1,0:T(8,128)(2,1)}, bf16[4,16,64,128]{3,2,1,0:T(8,128)(2,1)}) custom-call(s32[32]{0:T(128)} %owner_h.1, s32[32]{0:T(128)} %slot_h.1, s32[16,32]{1,0:T(8,128)} %bitcast.5, s32[32]{0:T(128)} %hit_h.1, s32[32]{0:T(128)} %tail_h.1, bf16[64,1024]{1,0:T(8,128)(2,1)} %x_h.1, bf16[64,1024]{1,0:T(8,128)(2,1)} %z_h.1, ...), custom_call_target="tpu_custom_call" | custom-call | tf_op jit(solution)/shard_map/pallas_call | solution.py:643
  59.3 0.0 copy-start
  59.3 1.6 %copy.24 = bf16[64,1024]{1,0:T(8,128)(2,1)} copy(bf16[64,1024]{1,0:T(8,128)(2,1)} %get-tuple-element.6) | data formatting | bytes 262144
  60.9 0.0 copy-done
  60.9 0.7 %copy.25 = bf16[64,1024]{1,0:T(8,128)(2,1)} copy(bf16[64,1024]{1,0:T(8,128)(2,1)S(1)} %copy-done) | data formatting | bytes 262144
  61.6 2.3 %copy.26 = bf16[4,16,64,128]{3,2,1,0:T(8,128)(2,1)} copy(bf16[4,16,64,128]{3,2,1,0:T(8,128)(2,1)} %get-tuple-element.8) | data formatting | bytes 2097152
Async XLA Ops:
  59.3 1.6 %copy-start = (bf16[64,1024]{1,0:T(8,128)(2,1)S(1)}, bf16[64,1024]{1,0:T(8,128)(2,1)}, u32[]{:S(2)}) copy-start(bf16[64,1024]{1,0:T(8,128)(2,1)} %get-tuple-element.7) | copy-start | bytes 393220

commit v4 on v3

--- a/solution.py
+++ b/solution.py
@@ -278,6 +278,8 @@
     xw_s,
     log_s,
     acc_s,
+    add_s,
+    keep_s,
     kv_ss,
     kv_rs,
     st_ss,
@@ -479,6 +481,16 @@
             factor = jnp.where(seen, meet[:, u : u + 1], 0.0)
             total = total + decay * factor * fed[u : u + 1, :]
         acc_s[rows, :] = total
+        late = jnp.exp(running[TAIL - 1 : TAIL, :] - running) * fed
+        added = dot(late, b[rows, :].astype(jnp.float32), ((0,), (0,)), precision=highest)
+        add_s[k] = added.reshape(add_s.shape[1:])
+        last = dot(
+            log_s[rows, :],
+            jnp.ones((TAIL, b.shape[1]), jnp.float32),
+            ((0,), (0,)),
+            precision=highest,
+        )
+        keep_s[k] = jnp.exp(last)
         return carry
 
     lax.fori_loop(0, reqs, within, 0)
@@ -540,16 +552,8 @@
         energy = jnp.sum(gated * gated, axis=1, keepdims=True)
         normed = gated / jnp.sqrt(energy / width + 1e-05) * gain[...]
         ssd_o[rows, :] = normed.astype(jnp.bfloat16)
-        fed = jnp.exp(running[TAIL - 1 : TAIL, :] - running) * xw_s[rows, :]
-        added = dot(fed, b[rows, :].astype(jnp.float32), ((0,), (0,)), precision=highest)
-        last = dot(
-            log_s[rows, :],
-            jnp.ones((TAIL, start.shape[2]), jnp.float32),
-            ((0,), (0,)),
-            precision=highest,
-        )
-        kept = jnp.exp(last)[:, None, :] * start.astype(jnp.float32)
-        fin_o[k] = (kept + added.reshape(start.shape)).astype(jnp.bfloat16)
+        kept = keep_s[k][:, None, :] * start.astype(jnp.float32)
+        fin_o[k] = (kept + add_s[k]).astype(jnp.bfloat16)
         return carry
 
     pltpu.make_async_remote_copy(
@@ -638,6 +642,8 @@
         pltpu.VMEM((count, width), jnp.float32),
         pltpu.VMEM((count, heads), jnp.float32),
         pltpu.VMEM((count, width), jnp.float32),
+        pltpu.VMEM((reqs, heads, size, state), jnp.float32),
+        pltpu.VMEM((reqs, heads, state), jnp.float32),
     ] + [pltpu.SemaphoreType.DMA((k,)) for k in (n, n, n, n, n, n, n, n, m, m, 18)]
     scratch += [pltpu.SemaphoreType.DMA, pltpu.SemaphoreType.DMA]
     return pl.pallas_call(

time: 64 us -> 62.3 us (0.973)
  Pallas kernels: 58.7 us -> 56.9 us
    pallas_call x1, Pallas kernels: 58.7 us -> 56.9 us  [fused(): pl.pallas_call(functools.partial(layer, n, m), out_shape=(jax.ShapeDtypeS...]
where the time goes in v4:
time: 62.3 us; the launch traced here: 62.1 us
  Pallas kernels  56.9 us (91%)
  local copies, waits for them, and re-layouts  4.52 us (7%)
  between operations  0.66 us (1%)
    pallas_call x1, Pallas kernels, fused(): pl.pallas_call(functools.partial(layer, n, m), out_shape=(jax.ShapeDtypeS...  56.9 us
    unnamed x5, local copies, waits for them, and re-layouts  4.52 us

profile of v4, /device:TPU:3, one launch (start us, length us, event | category | flops | bytes accessed | tf_op | source)
XLA Modules:
  0.0 62.1 jit_solution(4678101491530704286)
XLA Ops:
  0.6 56.9 %shard_map.193 = (bf16[64,1024]{1,0:T(8,128)(2,1)}, bf16[64,1024]{1,0:T(8,128)(2,1)}, bf16[4,16,64,128]{3,2,1,0:T(8,128)(2,1)}) custom-call(s32[32]{0:T(128)} %owner_h.1, s32[32]{0:T(128)} %slot_h.1, s32[16,32]{1,0:T(8,128)} %bitcast.5, s32[32]{0:T(128)} %hit_h.1, s32[32]{0:T(128)} %tail_h.1, bf16[64,1024]{1,0:T(8,128)(2,1)} %x_h.1, bf16[64,1024]{1,0:T(8,128)(2,1)} %z_h.1, ...), custom_call_target="tpu_custom_call" | custom-call | tf_op jit(solution)/shard_map/pallas_call | solution.py:649
  57.5 0.0 copy-start
  57.6 1.6 %copy.24 = bf16[64,1024]{1,0:T(8,128)(2,1)} copy(bf16[64,1024]{1,0:T(8,128)(2,1)} %get-tuple-element.6) | data formatting | bytes 262144
  59.2 0.0 copy-done
  59.2 0.7 %copy.25 = bf16[64,1024]{1,0:T(8,128)(2,1)} copy(bf16[64,1024]{1,0:T(8,128)(2,1)S(1)} %copy-done) | data formatting | bytes 262144
  59.8 2.3 %copy.26 = bf16[4,16,64,128]{3,2,1,0:T(8,128)(2,1)} copy(bf16[4,16,64,128]{3,2,1,0:T(8,128)(2,1)} %get-tuple-element.8) | data formatting | bytes 2097152
Async XLA Ops:
  57.5 1.6 %copy-start = (bf16[64,1024]{1,0:T(8,128)(2,1)S(1)}, bf16[64,1024]{1,0:T(8,128)(2,1)}, u32[]{:S(2)}) copy-start(bf16[64,1024]{1,0:T(8,128)(2,1)} %get-tuple-element.7) | copy-start | bytes 393220
